TPU v7x, 128 devices: a whole 4x4x4 slice. The times are simulated.
128 devices in a mesh: ep: 16 (over x, z), tp: 8 (over y, core).
Axes of the slice: x: 4, y: 4, z: 4, core: 2. Of those that a mesh axis runs over, the one named last changes fastest.
Arguments:
- layer_input: float32 [16384, 1024], P(('ep', 'tp')), may hold values from -6 to 6
- lengths: int32 [16], replicated, may hold values from 1024 to 1024, as said below
- routes: int32 [16384, 8], replicated, may hold values from 0 to 31, all different within a row; in each aligned block of 128 rows (0 to 127, 128 to 255, ...) at most 48 rows name the same one
- norm_gain: float32 [1024], replicated, may hold values from 0.5 to 1.5
- w_query: bfloat16 [1024, 1024], P(None, 'tp'), may hold values from -0.1875 to 0.1875
- w_keyval: bfloat16 [1024, 8, 128], P(None, 'tp'), may hold values from -0.1875 to 0.1875
- query_gain: float32 [1024], P('tp'), may hold values from 0.5 to 1.5
- key_gain: float32 [512], P('tp'), may hold values from 0.5 to 1.5
- w_out: bfloat16 [1024, 1024], P('tp'), may hold values from -3.5 to 3.5
- mlp_gain: float32 [1024], replicated, may hold values from 0.5 to 1.5
- w_router: float32 [1024, 32], replicated, may hold values from -0.09375 to 0.09375
- w_gate: bfloat16 [32, 1024, 512], P('ep', None, 'tp'), may hold values from -0.1875 to 0.1875
- w_up: bfloat16 [32, 1024, 512], P('ep', None, 'tp'), may hold values from -0.1875 to 0.1875
- w_down: bfloat16 [32, 512, 1024], P('ep', 'tp'), may hold values from -0.75 to 0.75
- cotangent: float32 [16384, 1024], P(('ep', 'tp')), may hold values from -6 to 6
Outputs:
- output: float32 [16384, 1024], P(('ep', 'tp'))
- grad_input: float32 [16384, 1024], P(('ep', 'tp'))
- loss: float32 [], replicated
- grad_norm_gain: float32 [1024], replicated
- grad_query: float32 [1024, 1024], P(None, 'tp')
- grad_keyval: float32 [1024, 8, 128], P(None, 'tp')
- grad_query_gain: float32 [1024], P('tp')
- grad_key_gain: float32 [512], P('tp')
- grad_out: float32 [1024, 1024], P('tp')
- grad_mlp_gain: float32 [1024], replicated
- grad_router: float32 [1024, 32], replicated
- grad_gate: float32 [32, 1024, 512], P('ep', None, 'tp')
- grad_up: float32 [32, 1024, 512], P('ep', None, 'tp')
- grad_down: float32 [32, 512, 1024], P('ep', 'tp')
Inputs may be any that keep to these rules, and one draw needn't show every extreme that they name: `lengths`: each group's slots hold one sequence from place 0, of the given length; the rest are padding; some group is full. Each token names 8 different experts; among the routes of the 128 tokens of one device no expert is named more than 48 times, a bound that some block reaches.
All inputs are finite; a program needn't handle non-finite values.
Results may differ from a plain program's by a relative error of at most 0.028.
Values may be sent and summed in bfloat16 or wider, within the bound.
A program may use at most 128 MiB of HBM per device.

v0:
```python
import jax
import jax.numpy as jnp
import numpy as np
from jax import lax
from jax.experimental import pallas as pl
from jax.experimental.pallas import tpu as pltpu
from jax.sharding import PartitionSpec as P

MESH = pl.DeviceIdType.MESH
f32, bf16 = jnp.float32, jnp.bfloat16
HEAD_DIM = 64
epsilon = 1e-06
masked_score = -1e30
highest = lax.Precision.HIGHEST
MIB = 2**20

X, Y, Z, C = (1, 0, 0, 0), (0, 1, 0, 0), (0, 0, 1, 0), (0, 0, 0, 1)
XM, YM, ZM = (-1, 0, 0, 0), (0, -1, 0, 0), (0, 0, -1, 0)
X2, Z2 = (2, 0, 0, 0), (0, 0, 2, 0)
NEAR = (0, 1, -1, 2)


def times(d, k):
    return tuple(v * k for v in d)


class Bank:
    def __init__(self, first, size):
        self.first, self.size, self.used = first, size, 0

    def restart(self):
        self.used = 0
        return self

    def take(self):
        assert self.used < self.size
        self.used += 1
        return self.first + self.used - 1


class Net:
    def __init__(self, send_sems, recv_sems):
        self.ep, self.tp = lax.axis_index("ep"), lax.axis_index("tp")
        self.x, self.z = self.ep // 4, self.ep % 4
        self.y, self.c = self.tp // 2, self.tp % 2
        self.send_sems, self.recv_sems = send_sems, recv_sems
        self.free = list(range(SENDS))
        self.unsent = {}
        self.group = None

    def device(self, d):
        x, y = (self.x + d[0]) % 4, (self.y + d[1]) % 4
        z, c = (self.z + d[2]) % 4, (self.c + d[3]) % 2
        return (x * 4 + z, y * 2 + c)

    def ep_at(self, dx, dz):
        return ((self.x + dx) % 4) * 4 + (self.z + dz) % 4

    def tp_at(self, dy, dc):
        return ((self.y + dy) % 4) * 2 + (self.c + dc) % 2

    def barrier(self, dirs):
        sem = pltpu.get_barrier_semaphore()
        for d in dirs:
            pl.semaphore_signal(sem, inc=1, device_id=self.device(d), device_id_type=MESH)
        pl.semaphore_wait(sem, len(dirs))

    def send(self, src, dst, d, bank):
        i = self.free.pop(0)
        copy = pltpu.make_async_remote_copy(
            src_ref=src,
            dst_ref=dst,
            send_sem=self.send_sems.at[i],
            recv_sem=self.recv_sems.at[bank.take()],
            device_id=self.device(d),
            device_id_type=MESH,
        )
        copy.start()
        self.unsent.setdefault(self.group, []).append((copy, i))
        return copy

    def keep(self, src, dst):
        i = self.free.pop(0)
        copy = pltpu.make_async_copy(src, dst, self.send_sems.at[i])
        copy.start()
        return copy, i

    def kept(self, pair):
        pair[0].wait()
        self.free.append(pair[1])

    def sent(self, copy):
        for group, pairs in self.unsent.items():
            for _, i in [pair for pair in pairs if pair[0] is copy]:
                copy.wait_send()
                self.free.append(i)
            self.unsent[group] = [pair for pair in pairs if pair[0] is not copy]

    def finish(self, *groups):
        for group in groups or tuple(self.unsent):
            for copy, i in self.unsent.pop(group, ()):
                copy.wait_send()
                self.free.append(i)


class GatherTp:
    def __init__(self, net, bank, ref, own=None):
        self.net, self.bank, self.ref = net, bank.restart(), ref
        self.own = own or (lambda half: ref(net.tp, half))
        self.copies = {}
        self.done = set()

    def wait(self, *key):
        if key not in self.done:
            self.done.add(key)
            self.copies[key].wait_recv()

    def along(self, dy, half, sign):
        src = self.own(half) if dy == 0 else self.ref(self.net.tp_at(dy, 0), half)
        to = (dy - sign + 1) % 4 - 1
        self.copies[("y", to, half)] = self.net.send(
            src, self.ref(self.net.tp_at(dy, 0), half), times(Y, sign), self.bank
        )

    def across(self, dy):
        for half in (0, 1):
            src = self.own(half) if dy == 0 else self.ref(self.net.tp_at(dy, 0), half)
            self.copies[("c", dy, half)] = self.net.send(
                src, self.ref(self.net.tp_at(dy, 0), half), C, self.bank
            )

    def start(self):
        self.along(0, 0, 1)
        self.along(0, 1, -1)
        self.along(0, 1, 1)
        self.along(0, 0, -1)
        self.across(0)

    def relay(self):
        self.wait("y", -1, 0)
        self.along(-1, 0, 1)
        self.wait("y", 1, 1)
        self.along(1, 1, -1)

    def share(self):
        for dy, half in ((-1, 1), (1, 0)):
            self.wait("y", dy, half)
            self.across(dy)

    def spread(self):
        for half in (0, 1):
            self.wait("y", 2, half)
        self.across(2)

    def need(self, dy, dc):
        if dc:
            for half in (0, 1):
                self.wait("c", dy, half)
        elif dy:
            for half in (0, 1):
                self.wait("y", dy, half)

    def finish(self):
        for key in list(self.copies):
            self.wait(*key)


class ScatterTp:
    def __init__(self, net, bank, ref, sib, far, near):
        self.bank = bank.restart()
        self.net, self.ref, self.sib, self.far_at, self.near_at = net, ref, sib, far, near
        self.copies = {}

    def across(self, dy):
        i = NEAR.index(dy)
        for half in (0, 1):
            self.copies[("c", dy, half)] = self.net.send(
                self.ref(self.net.tp_at(dy, 1), half), self.sib(i, half), C, self.bank
            )

    def join(self, dy, half):
        self.copies[("c", dy, half)].wait_recv()
        return self.ref(self.net.tp_at(dy, 0), half)[...] + self.sib(NEAR.index(dy), half)[...]

    def far(self):
        for half, sign in ((0, 1), (1, -1)):
            ref = self.ref(self.net.tp_at(2, 0), half)
            ref[...] = self.join(2, half)
            self.copies[("f", half)] = self.net.send(ref, self.far_at(half), times(Y, sign), self.bank)

    def towards(self, part, half):
        sign = (1, -1)[part]
        ref = self.ref(self.net.tp_at(sign, 0), half)
        total = self.join(sign, half)
        if half == part:
            self.copies[("f", part)].wait_recv()
            total = total + self.far_at(part)[...]
        ref[...] = total
        self.copies[("n", part, half)] = self.net.send(
            ref, self.near_at(part, half), times(Y, sign), self.bank
        )

    def near_first(self):
        for part in (0, 1):
            self.towards(part, 1 - part)

    def near_second(self):
        for part in (0, 1):
            self.towards(part, part)

    def last(self, half):
        total = self.join(0, half).astype(f32)
        for part in (0, 1):
            self.copies[("n", part, half)].wait_recv()
            total = total + self.near_at(part, half)[...].astype(f32)
        return total


class GatherEp:
    def __init__(self, net, bank, buf, rows):
        self.bank = bank.restart()
        self.net, self.buf, self.rows = net, buf, rows
        self.copies = {}
        self.done = set()

    def ref(self, h, j, k, part):
        half, quarter = self.rows // 2, self.rows // 4
        e = self.net.ep_at(j, k) if h == 0 else self.net.ep_at(k, j)
        if part is None:
            return self.buf.at[e, pl.ds(h * half, half)]
        return self.buf.at[e, pl.ds(h * half + part * quarter, quarter)]

    def send(self, h, j, k, part, along, sign):
        d = (X, Z)[along if h == 0 else 1 - along]
        r = self.ref(h, j, k, part)
        to = (j - sign, k) if along == 0 else (j, k - sign)
        to = tuple((v + 1) % 4 - 1 for v in to)
        self.copies[(h, *to, part)] = self.net.send(r, r, times(d, sign), self.bank)

    def wait(self, *key):
        if key not in self.done:
            self.done.add(key)
            self.copies[key].wait_recv()

    def need(self, h, j, k):
        if (j, k) != (0, 0):
            for part in (None,) if (h, j, k, None) in self.copies else (0, 1):
                self.wait(h, j, k, part)

    def block(self, dx, dz):
        self.need(0, dx, dz)
        self.need(1, dz, dx)

    def start(self):
        for along in (0, 1):
            for h in (0, 1):
                for sign in (1, -1):
                    self.send(h, 0, 0, None, along, sign)

    def first(self):
        for part, sign in ((0, 1), (1, -1)):
            for h in (0, 1):
                self.wait(h, -sign, 0, None)
                self.send(h, -sign, 0, part, 0, sign)
        for sign in (1, -1):
            for h in (0, 1):
                for turn in (1, -1):
                    self.send(h, -sign, 0, None, 1, turn)

    def far(self):
        for h in (0, 1):
            self.need(h, 2, 0)
            for turn in (1, -1):
                self.send(h, 2, 0, None, 1, turn)

    def second(self, j):
        for part, sign in ((0, 1), (1, -1)):
            for h in (0, 1):
                self.wait(h, j, -sign, None)
                self.send(h, j, -sign, part, 1, sign)

    def finish(self):
        for key in list(self.copies):
            self.wait(*key)


class ScatterEp:
    def __init__(self, net, bank, term, landed, rows):
        self.bank = bank.restart()
        self.net, self.term, self.landed, self.rows = net, term, landed, rows
        self.copies = {}

    def ref(self, h, g, j, part):
        j, k = (j, NEAR[g]) if g < 4 else (0, j)
        half, quarter = self.rows // 2, self.rows // 4
        e = self.net.ep_at(k, j) if h == 0 else self.net.ep_at(j, k)
        if part is None:
            return self.term(e, h * half, half)
        return self.term(e, h * half + part * quarter, quarter)

    def slot(self, g, h, which, part=None):
        half, quarter = self.rows // 2, self.rows // 4
        i = (g * 2 + h) * 3 + which
        return self.landed(i, 0, half) if part is None else self.landed(i, part * quarter, quarter)

    def dir(self, h, g, sign):
        return times((Z, X)[(g == 4) if h == 0 else (g != 4)], sign)

    def far(self, g):
        for h in (0, 1):
            for part, sign in ((0, 1), (1, -1)):
                self.copies[(g, h, 2, part)] = self.net.send(
                    self.ref(h, g, 2, part), self.slot(g, h, 2, part), self.dir(h, g, sign), self.bank
                )

    def near(self, g):
        for h in (0, 1):
            for part, sign in ((0, 1), (1, -1)):
                self.copies[(g, h, 2, part)].wait_recv()
                r = self.ref(h, g, sign, part)
                r[...] = r[...] + self.slot(g, h, 2, part)[...]
                self.copies[(g, h, part)] = self.net.send(
                    self.ref(h, g, sign, None), self.slot(g, h, part), self.dir(h, g, sign), self.bank
                )

    def last(self, g, h):
        for part in (0, 1):
            self.copies[(g, h, part)].wait_recv()
        total = self.ref(h, g, 0, None)[...].astype(f32)
        for part in (0, 1):
            total = total + self.slot(g, h, part)[...].astype(f32)
        return total

    def turn(self, g):
        for h in (0, 1):
            self.ref(h, g, 0, None)[...] = self.last(g, h).astype(bf16)


def lanes(shape):
    return lax.broadcasted_iota(jnp.int32, shape, len(shape) - 1)


def low(shape):
    return lanes(shape) < HEAD_DIM


def normed(v):
    factor = lax.rsqrt(jnp.mean(v * v, -1, keepdims=True) + epsilon)
    return v * factor, factor


def norm_back(grad, hat, factor):
    return factor * (grad - hat * jnp.mean(grad * hat, -1, keepdims=True))


def pair_sums(v):
    first = low(v.shape)
    a = jnp.sum(jnp.where(first, v, 0.0), -1, keepdims=True)
    b = jnp.sum(jnp.where(first, 0.0, v), -1, keepdims=True)
    return jnp.where(first, a, b)


def pair_normed(v):
    factor = lax.rsqrt(pair_sums(v * v) / HEAD_DIM + epsilon)
    return v * factor, factor


def pair_norm_back(grad, hat, factor):
    return factor * (grad - hat * (pair_sums(grad * hat) / HEAD_DIM))


def partner(v):
    half = HEAD_DIM // 2
    return jnp.where(
        lanes(v.shape) % HEAD_DIM < half, pltpu.roll(v, 128 - half, 1), pltpu.roll(v, half, 1)
    )


def rotate(v, cosine, sine):
    return v * cosine + partner(v) * sine


def rotate_back(v, cosine, sine):
    return v * cosine - partner(v) * sine


def swap(v):
    return pltpu.roll(v, HEAD_DIM, v.ndim - 1)


def dot(a, b):
    return jnp.dot(a, b, preferred_element_type=f32)


def dot_nt(a, b):
    return lax.dot_general(a, b, (((1,), (1,)), ((), ())), preferred_element_type=f32)


def dot_tn(a, b):
    return lax.dot_general(a, b, (((0,), (0,)), ((), ())), preferred_element_type=f32)


def rotary(length):
    half = HEAD_DIM // 2
    frequency = 10000.0 ** (-(np.arange(half, dtype=np.float64) * 2.0 / HEAD_DIM))
    angles = np.arange(length, dtype=np.float64)[:, None] * frequency[None, :]
    cosine, sine = np.cos(angles), np.sin(angles)
    cosine = np.concatenate([cosine] * 4, -1).astype(np.float32)
    sine = np.concatenate([-sine, sine] * 2, -1).astype(np.float32)
    return cosine, sine


VM = pl.BlockSpec(memory_space=pltpu.VMEM)
SM = pl.BlockSpec(memory_space=pltpu.SMEM)
ANY = pl.BlockSpec(memory_space=pl.ANY)


def shaped(shape, dtype):
    return jax.ShapeDtypeStruct(shape, dtype)


def params(collective_id, vmem):
    return pltpu.CompilerParams(
        collective_id=collective_id, has_side_effects=True, vmem_limit_bytes=int(vmem * MIB)
    )


def key_value(qkv, q_gain, k_gain, cosine, sine):
    q_hat, _ = pair_normed(qkv[:, :128])
    kv = qkv[:, 128:]
    first = low(kv.shape)
    other = swap(kv)
    k_raw = jnp.where(first, kv, other)
    k_hat, _ = pair_normed(k_raw)
    query = (rotate(q_hat * q_gain, cosine, sine).astype(bf16).astype(f32) * HEAD_DIM**-0.5).astype(bf16)
    key = rotate(k_hat * k_gain, cosine, sine).astype(bf16)
    value = jnp.where(first, other, kv).astype(bf16)
    value = jnp.concatenate([value, jnp.ones_like(value)], -1)
    return query, key, value, qkv[:, :128], k_raw


class Exchange:
    def __init__(self, net, bank, out, half_way, got):
        self.bank = bank.restart()
        self.net, self.out, self.half_way, self.got = net, out, half_way, got

    def start(self):
        net = self.net
        self.first = [
            net.send(self.out.at[(net.x + k) % 4], self.half_way.at[net.x], times(X, k), self.bank)
            for k in (1, -1, 2)
        ]
        self.half_way[net.x] = self.out[net.x]

    def turn(self):
        net = self.net
        for copy in self.first:
            copy.wait_recv()
        self.second = [
            net.send(self.half_way.at[:, (net.z + k) % 4], self.got.at[:, net.z], times(Z, k), self.bank)
            for k in (1, -1, 2)
        ]
        self.got[:, net.z] = self.half_way[:, net.z]

    def finish(self):
        for copy in self.second:
            copy.wait_recv()


class AxisSum:
    def __init__(self, net, bank, term, slots, steps):
        self.net, self.term, self.slots = net, term, slots
        self.copies = [net.send(term, slots.at[i], d, bank) for i, d in enumerate(steps)]

    def finish(self):
        total = self.term[...]
        for i, copy in enumerate(self.copies):
            copy.wait_recv()
            total = total + self.slots[i]
            self.net.sent(copy)
        return total


ALONG_X, ALONG_Y, ALONG_Z = ([times(d, k) for k in (1, -1, 2)] for d in (X, Y, Z))
Y2 = times(Y, 2)

SENDS = 232
BANKS = {"ep0": 40, "ep1": 40, "ep2": 40, "tp0": 14, "tp1": 14}
BANKS |= {name + str(a): 14 for name in ("gather", "scatter") for a in range(3)}
BANKS |= {"gates": 6, "back": 6, "small": 11, "gains": 10}

ORDER = (
    (0, 0), (-1, 0), (1, 0), (0, -1),
    (0, 1), (2, 0), (0, 2), (-1, -1),
    (-1, 1), (1, -1), (1, 1), (2, -1),
    (2, 1), (-1, 2), (1, 2), (2, 2),
)
BATCH = 8


def layer_kernel(*refs, inputs, outputs, scratch):
    names = inputs + outputs + scratch
    r = dict(zip(names, refs, strict=True))

    class R:
        pass

    v = R()
    for name, ref in r.items():
        setattr(v, name, ref)
    v.totals, v.q_raw, v.d_key_t = v.grad_query, v.grad_keyval, v.grad_out
    v.d_value_t, v.x, v.cot_f = v.grad_gate, v.grad_up, v.grad_down
    net = Net(v.send_sems, v.recv_sems)
    banks, first = {}, 0
    for name, size in BANKS.items():
        banks[name] = Bank(first, size)
        first += size
    rows, width = v.output.shape
    half_rows = rows // 2
    group = rows * 8
    units = v.w_down.shape[1]
    ff = units * 8
    n_exp = v.w_router_t.shape[0]
    slots = v.places.shape[1] // 2
    full = 16 * slots
    seq_len = v.lengths[net.ep]
    factor = HEAD_DIM**-0.5

    def weight(a, j, t):
        return v.w.at[j, pl.ds(pl.multiple_of(a * ff + t * units, units), units)]

    def rows_of(i, count=1):
        return pl.ds(pl.multiple_of(i * rows, rows), rows * count)

    def half_of(t, half):
        return pl.ds(pl.multiple_of(t * rows + half * half_rows, half_rows), half_rows)

    x_load = [net.keep(v.layer_input.at[pl.ds(i * half_rows, half_rows)], v.x.at[i]) for i in (0, 1)]
    early = [
        net.keep(v.w_query, v.w_qkv.at[:, pl.ds(0, 128)]),
        net.keep(v.w_keyval, v.w_qkv.at[:, pl.ds(128, 128)]),
        net.keep(v.cosine_in, v.cosine),
        net.keep(v.sine_in, v.sine),
    ]
    cot_load = [net.keep(v.cotangent.at[pl.ds(i * half_rows, half_rows)], v.cot_f.at[i]) for i in (0, 1)]
    weight_loads = [
        net.keep(source.at[j], weight(a, j, net.tp))
        for a, source in enumerate((v.w_gate, v.w_up, v.w_down))
        for j in (0, 1)
    ]
    late = [net.keep(v.routes_in, v.routes), net.keep(v.w_out_in, v.w_out)]
    net.barrier([X, XM, X2, Y, YM, Y2, Z, ZM, Z2, C])

    for copy in x_load:
        net.kept(copy)
    x_hat, _ = normed(v.x[...].reshape(rows, width))
    v.spare[rows_of(net.tp), :] = (x_hat * v.norm_gain[...]).astype(bf16)
    tokens = GatherTp(net, banks["tp0"], lambda t, half: v.spare.at[half_of(t, half)])
    tokens.start()
    place = net.tp * rows + lax.broadcasted_iota(jnp.int32, (rows, 1), 0)
    for copy in cot_load:
        net.kept(copy)
    v.cot[net.ep] = jnp.where(place < seq_len, v.cot_f[...].reshape(rows, width), 0.0).astype(bf16)
    cots = GatherEp(net, banks["ep0"], v.cot, rows)
    net.group = "cot"
    cots.start()
    net.group = None

    for copy in early + late:
        net.kept(copy)
    v.k_gain[:, 0:HEAD_DIM] = v.key_gain[...]
    k_gain = v.k_gain[...]
    k_gain = jnp.where(low(k_gain.shape), k_gain, swap(k_gain))
    q_gain = v.query_gain[...]

    def project(dy):
        at = rows_of(net.tp_at(dy, 0) - net.c, 2)
        h = v.spare[at, :]
        parts = key_value(dot(h, v.w_qkv[...]), q_gain, k_gain, v.cosine[at, :], v.sine[at, :])
        for ref, part in zip((v.query, v.key, v.value, v.q_raw, v.k_raw), parts, strict=True):
            ref[at, :] = part
        v.h_t[:, at] = h.T

    def routing():
        for s in range(16):
            segment = v.routes[:, rows_of(s * 8 + net.tp)]
            for j in (0, 1):
                same = (segment == net.ep * 2 + j).astype(f32)
                v.hits[2 * s + j : 2 * s + j + 1, :] = jnp.max(same, 0, keepdims=True)
        before = lax.broadcasted_iota(jnp.int32, (rows, rows), 0) < lanes((rows, rows))
        rank = dot(v.hits[...].astype(bf16), before.astype(bf16))
        rank = jnp.where(v.hits[...] > 0.5, rank, -1.0)
        slot = lax.broadcasted_iota(jnp.int32, (slots, rows), 0).astype(f32)
        for s in range(16):
            for j in (0, 1):
                mine = rank[2 * s + j : 2 * s + j + 1]
                v.places[s, j * slots : (j + 1) * slots, :] = (slot == mine).astype(bf16)

    def count():
        v.counted[...] = jnp.zeros_like(v.counted)

        def one(g, _):
            segment = v.routes[:, pl.ds(pl.multiple_of(g * group, group), group)]
            segment = jnp.where(lanes(segment.shape) < v.lengths[g], segment, -1)
            for e in range(n_exp):
                hit = (segment == e).astype(f32)
                total = hit[:, 0:128]
                for i in range(1, group // 128):
                    total = total + hit[:, i * 128 : (i + 1) * 128]
                v.counted[e] += total
            return 0

        lax.fori_loop(0, 16, one, 0)

    routing()
    count()
    tokens.need(0, 1)
    project(0)
    tokens.relay()
    cots_step = lambda step, *a: (setattr(net, "group", "cot"), step(*a), setattr(net, "group", None))
    cots_step(cots.first)
    tokens.share()
    cots_step(cots.second, 0)
    tokens.need(-1, 1)
    project(-1)
    tokens.need(1, 1)
    project(1)
    cots_step(cots.far)
    tokens.spread()
    for copy in weight_loads:
        net.kept(copy)
    w_step = lambda step, *a: (setattr(net, "group", "w"), step(*a), setattr(net, "group", None))
    gate, up, down = (
        GatherTp(net, banks[f"gather{a}"], lambda t, half, a=a: weight(a, half, t)) for a in range(3)
    )
    w_step(gate.start)
    w_step(up.start)
    tokens.need(2, 1)
    project(2)
    tokens.finish()

    bias = jnp.where(lanes((1, group)) < seq_len, 0.0, masked_score)

    def weights_of(q, head):
        q_head = jnp.where(low(q.shape) == (head == 0), q, jnp.zeros_like(q))
        return jnp.exp(dot_nt(q_head, v.key[...]) + bias).astype(bf16)

    def attend(dy):
        def one(i, _):
            t = net.tp_at(dy, 1 - i)
            at = rows_of(t)
            q = v.query[at, :]
            first = low(q.shape)
            mixed = [dot(weights_of(q, head), v.value[...]) for head in (0, 1)]
            total = jnp.where(first, mixed[0][:, 128:], mixed[1][:, 128:])
            o = (jnp.where(first, mixed[0][:, :128], mixed[1][:, :128]) / total).astype(bf16)
            v.attn_o[at, :] = o
            v.totals[at, :] = total
            v.spare[rows_of(8 + t), :] = dot(o, v.w_out[...]).astype(bf16)
            return 0

        lax.fori_loop(0, 2, one, 0)

    def token_sums():
        return ScatterTp(
            net,
            banks["tp1"],
            lambda t, half: v.spare.at[half_of(8 + t, half)],
            lambda i, half: v.from_sib.at[i, pl.ds(half * half_rows, half_rows)],
            lambda half: v.from_far.at[half],
            lambda part, half: v.from_near.at[part, pl.ds(half * half_rows, half_rows)],
        )

    sums = token_sums()
    attend(2)
    sums.across(2)
    attend(1)
    sums.across(1)
    sums.far()
    attend(-1)
    sums.across(-1)
    cots_step(cots.second, -1)
    sums.near_first()
    attend(0)
    sums.across(0)
    w_step(gate.relay)
    sums.near_second()
    cots_step(cots.second, 1)
    cots_step(cots.second, 2)
    h_mid = v.output
    for half in (0, 1):
        at = pl.ds(half * half_rows, half_rows)
        h_mid[at, :] = v.x[half] + sums.last(half)
    net.finish(None)

    h_hat, h_scale = normed(h_mid[...])
    mlp_in = h_hat * v.mlp_gain[...]
    v.tok[net.ep] = mlp_in.astype(bf16)
    tokens = GatherEp(net, banks["ep1"], v.tok, rows)
    tokens.start()
    w_step(down.start)
    w_step(gate.share)
    w_step(up.relay)

    w_router_t = v.w_router_t
    logits = lax.dot_general(
        w_router_t[...], mlp_in, (((1,), (1,)), ((), ())), precision=highest, preferred_element_type=f32
    )
    token_at = net.tp * rows + lanes((1, rows))
    valid = jnp.where(token_at < seq_len, 1.0, 0.0)
    expert = lax.broadcasted_iota(jnp.int32, (n_exp, rows), 0)
    mine = v.routes[:, rows_of(net.ep * 8 + net.tp)]
    chosen = expert == mine[0:1]
    for k in range(1, mine.shape[0]):
        chosen = jnp.logical_or(chosen, expert == mine[k : k + 1])
    top = jnp.max(logits, 0, keepdims=True)
    weights = jnp.exp(logits - top)
    probs = weights / jnp.sum(weights, 0, keepdims=True)
    top = jnp.max(jnp.where(chosen, logits, masked_score), 0, keepdims=True)
    weights = jnp.where(chosen, jnp.exp(jnp.where(chosen, logits - top, 0.0)), 0.0)
    soft = weights / jnp.sum(weights, 0, keepdims=True)
    v.probs[...] = probs
    v.soft[...] = soft
    gates = soft * valid
    for e in range(16):
        v.gate_out[e // 4, e % 4, 0:2, :] = gates[2 * e : 2 * e + 2]
    to_owners = Exchange(net, banks["gates"], v.gate_out, v.gate_mid, v.gate_got)
    to_owners.start()

    cots.finish()
    net.finish("cot")
    tokens.first()
    w_step(up.share)
    w_step(gate.spread)
    to_owners.turn()
    tokens.second(0)
    w_step(down.relay)
    w_step(up.spread)
    tokens.far()
    w_step(down.share)
    to_owners.finish()
    tokens.second(-1)
    tokens.second(1)
    w_step(down.spread)
    tokens.second(2)
    for gather in (gate, up, down):
        gather.finish()
    net.finish("w")

    n = BATCH * slots

    def picked(j, at, count):
        return pl.ds(pl.multiple_of(j * full + at, slots), count)

    def d_picked(j, at, count):
        return pl.ds(pl.multiple_of((2 + j) * full + at, slots), count)

    def batch(b):
        members = []
        for i, (dx, dz) in enumerate(ORDER[b * BATCH : (b + 1) * BATCH]):
            tokens.block(dx, dz)
            s = net.ep_at(dx, dz)
            members.append((s, (net.x + dx) % 4, (net.z + dz) % 4))
            here = v.places[s]
            taken = dot(here, v.tok[s]).astype(bf16)
            taken_d = dot(here, v.cot[s]).astype(bf16)
            for j in (0, 1):
                v.big[picked(j, b * n + i * slots, slots), :] = taken[j * slots : (j + 1) * slots]
                v.big[d_picked(j, b * n + i * slots, slots), :] = taken_d[j * slots : (j + 1) * slots]

        def one(j, _):
            at, at_d = picked(j, b * n, n), d_picked(j, b * n, n)
            gate_col = []
            for s, sx, sz in members:
                here = v.places[s, pl.ds(pl.multiple_of(j * slots, slots), slots), :].astype(f32)
                gate_col.append(jnp.sum(here * v.gate_got[sx, sz, pl.ds(j, 1), :], -1, keepdims=True))
            gate_col = jnp.concatenate(gate_col, 0)
            pre = dot_nt(v.big[at, :], v.w[j, 0 : 2 * ff])
            d_hidden = dot_nt(v.big[at_d, :], v.w[j, 2 * ff :])
            g, u = pre[:, :ff], pre[:, ff:]
            sigma = 0.5 * jnp.tanh(0.5 * g) + 0.5
            act = g * sigma
            hid = act * u
            d_gate = jnp.sum(d_hidden * hid, -1, keepdims=True)
            hid = (gate_col * hid).astype(bf16)
            v.deep[pl.ds(2 * full + b * n, n), pl.ds(pl.multiple_of(j * ff, ff), ff)] = hid
            d_hidden = d_hidden * gate_col
            v.deep[at, 0:ff] = (d_hidden * u * (sigma * (1.0 + g - act))).astype(bf16)
            v.deep[at, ff:] = (d_hidden * act).astype(bf16)
            v.spare[picked(j, b * n, n), :] = dot(hid, v.w[j, 2 * ff :]).astype(bf16)
            v.row_back[j] = dot(v.deep[at, :], v.w[j, 0 : 2 * ff]).astype(bf16)
            for i, (s, sx, sz) in enumerate(members):
                here = v.places[s, pl.ds(pl.multiple_of(j * slots, slots), slots), :].astype(f32)
                d = jnp.sum(here * d_gate[i * slots : (i + 1) * slots], 0, keepdims=True)
                v.back_out[sx, sz, pl.ds(j, 1), :] = d
            return 0

        lax.fori_loop(0, 2, one, 0)
        for i, (s, _, _) in enumerate(members):
            at = pl.ds(i * slots, slots)
            both = jnp.concatenate([v.row_back[0, at, :], v.row_back[1, at, :]], 0)
            v.cot[s] = dot_tn(v.places[s], both).astype(bf16)

    row_sums = ScatterEp(
        net,
        banks["ep0"],
        lambda e, start, count: v.cot.at[e, pl.ds(start, count)],
        lambda i, start, count: v.landed.at[i, pl.ds(start, count)],
        rows,
    )
    batch(0)
    tokens.finish()
    net.finish(None)
    row_sums.far(0)
    batch(1)

    to_tokens = Exchange(net, banks["back"], v.back_out, v.back_mid, v.back_got)
    to_tokens.start()
    mix_sums = ScatterEp(
        net,
        banks["ep1"],
        lambda e, start, count: v.big.at[pl.ds(pl.multiple_of(e * rows + start, 16), count)],
        lambda i, start, count: v.tok.at[i // 2, pl.ds(i % 2 * half_rows + start, count)],
        rows,
    )
    for g in (3, 1, 2):
        row_sums.far(g)
    row_sums.near(0)

    def grads(j, _):
        v.w[j, 0 : 2 * ff] = dot_tn(
            v.deep[picked(j, 0, full), :], v.big[picked(j, 0, full), :]
        ).astype(bf16)
        hidden = v.deep[2 * full : 3 * full, pl.ds(pl.multiple_of(j * ff, ff), ff)]
        v.w[j, 2 * ff :] = dot_tn(hidden, v.big[d_picked(j, 0, full), :]).astype(bf16)
        return 0

    lax.fori_loop(0, 2, grads, 0)
    to_tokens.turn()
    for g in (3, 1, 2):
        row_sums.near(g)
    gate, up, down = (
        ScatterTp(
            net,
            banks[f"scatter{a}"],
            lambda t, half, a=a: weight(a, half, t),
            lambda i, half, a=a: v.w_sib.at[i, a, half],
            lambda half, a=a: v.w_far.at[a, half],
            lambda part, half, a=a: v.w_near.at[part, a, half],
        )
        for a in range(3)
    )
    for dy in (2, 1, -1, 0):
        for sum_ in (gate, up, down):
            w_step(sum_.across, dy)
    for s in range(16):
        i = net.ep_at(*ORDER[s])
        both = jnp.concatenate([v.spare[picked(j, s * slots, slots), :] for j in (0, 1)], 0)
        v.big[rows_of(i), :] = dot_tn(v.places[i], both).astype(bf16)
    row_sums.turn(3)
    row_sums.far(4)
    for sum_ in (gate, up, down):
        w_step(sum_.far)
    to_tokens.finish()

    for e in range(16):
        v.d_gates[2 * e : 2 * e + 2, :] = v.back_got[e // 4, e % 4, 0:2, :]
    probs, soft = v.probs[...], v.soft[...]
    d_gates = v.d_gates[...] * valid
    d_chosen = soft * (d_gates - jnp.sum(soft * d_gates, 0, keepdims=True))
    nvalid = jnp.int32(0)
    for e in range(16):
        nvalid = nvalid + v.lengths[e]
    nvalid = nvalid.astype(f32)
    counts = jnp.sum(jnp.sum(v.counted[...], 1), -1, keepdims=True)
    balance = n_exp * counts / (8 * nvalid * nvalid)
    d_logits = d_chosen + valid * probs * (balance - jnp.sum(probs * balance, 0, keepdims=True))
    d_mlp_in = lax.dot_general(
        d_logits, w_router_t[...], (((0,), (0,)), ((), ())), precision=highest, preferred_element_type=f32
    )
    h_hat, h_scale = normed(h_mid[...])
    mlp_in = h_hat * v.mlp_gain[...]
    small = v.small
    small[0:n_exp, :] = jnp.dot(d_logits, mlp_in, precision=highest, preferred_element_type=f32)
    small[n_exp + 8 :, :] = jnp.zeros((8, width), f32)
    small[n_exp + 8 :, 0:n_exp] = lax.dot_general(
        valid + jnp.zeros((8, rows), f32), probs, (((1,), (1,)), ((), ())), precision=highest, preferred_element_type=f32
    )
    row_sums.turn(1)
    row_sums.turn(2)
    row_sums.near(4)
    row_sums.turn(0)
    d_out = jnp.where(place < seq_len, v.cot_f[...].reshape(rows, width), 0.0)
    total = jnp.concatenate([row_sums.last(4, 0), row_sums.last(4, 1)], 0)
    d_mlp_in = d_mlp_in + total
    gain_grad = jnp.sum(d_mlp_in * h_hat, 0, keepdims=True)
    small[n_exp : n_exp + 8, :] = gain_grad + jnp.zeros((8, width), f32)
    d_mid = v.grad_input
    d_mid[...] = d_out + norm_back(d_mlp_in * v.mlp_gain[...], h_hat, h_scale)

    net.finish(None)

    v.d_all[net.tp] = d_mid[...].astype(bf16)
    tokens = GatherTp(net, banks["tp0"], lambda t, half: v.d_all.at[t, pl.ds(half * half_rows, half_rows)])
    tokens.start()
    net.group = "mix"
    for g in (3, 1, 2, 0):
        mix_sums.far(g)
    net.group = None
    share = small.shape[0] // 2
    small_first = net.send(small, v.small_sib, C, banks["small"])
    v.d_key_t[...] = jnp.zeros_like(v.d_key_t)
    v.d_value_t[...] = jnp.zeros_like(v.d_value_t)

    def softmax_of(i, _):
        q = v.query[rows_of(i), :]
        for head in (0, 1):
            v.deep[rows_of(head * 8 + i), :] = weights_of(q, head)
        return 0

    lax.fori_loop(0, 8, softmax_of, 0)
    tokens.relay()
    small_first.wait_recv()
    net.sent(small_first)
    mine = pl.ds(pl.multiple_of(net.c * share, 8), share)
    small[mine, :] = small[mine, :] + v.small_sib[mine, :]
    net.group = "mix"
    for g in (3, 1, 2, 0):
        mix_sums.near(g)
    net.group = None
    tokens.share()
    tokens.spread()
    for sum_ in (gate, up, down):
        w_step(sum_.near_first)
        w_step(sum_.near_second)
    small_y = AxisSum(net, banks["small"], small.at[mine], v.small_got.at[0], ALONG_Y)
    tokens.finish()

    def back(i, _):
        at = rows_of(2 * i, 2)
        d_rows = jnp.concatenate([v.d_all[2 * i], v.d_all[2 * i + 1]], 0)
        d_o = dot_nt(d_rows, v.w_out[...]).astype(bf16).astype(f32) / v.totals[at, :]
        shift = pair_sums(d_o * v.attn_o[at, :].astype(f32))
        d_o = d_o.astype(bf16)
        q = v.query[at, :]
        first = low(q.shape)
        d_q = []
        for head in (0, 1):
            own = first == (head == 0)
            d_o_head = jnp.where(own, d_o, jnp.zeros_like(d_o))
            q_head = jnp.where(own, q, jnp.zeros_like(q))
            p = v.deep[rows_of(head * 8 + 2 * i, 2), :]
            d_p = dot_nt(d_o_head, v.value[:, 0:128]) - shift[:, head * HEAD_DIM : head * HEAD_DIM + 1]
            d_s = (p.astype(f32) * d_p).astype(bf16)
            d_q.append(dot(d_s, v.key[...]))
            v.d_key_t[...] += dot_tn(q_head, d_s)
            v.d_value_t[...] += dot_tn(d_o_head, p).reshape(v.d_value_t.shape)
        d_query = (jnp.where(first, d_q[0], d_q[1]) * factor).astype(bf16).astype(f32)
        d_gained = rotate_back(d_query, v.cosine[at, :], v.sine[at, :])
        hat, scale = pair_normed(v.q_raw[at, :])
        v.gain[8:9, :] += jnp.sum(d_gained * hat, 0, keepdims=True)
        v.d_qkv[at, 0:128] = pair_norm_back(d_gained * q_gain, hat, scale).astype(bf16)
        return 0

    v.gain[...] = jnp.zeros_like(v.gain)
    lax.fori_loop(0, 2, back, 0)
    blocks, block = v.grad_terms.shape[0], v.grad_terms.shape[1]
    grad_o = dot_tn(v.attn_o[...], v.d_all[...].reshape(group, width)).T
    for e in range(blocks):
        v.grad_terms[e, :, 256:384] = grad_o[e * block : (e + 1) * block].astype(bf16)
    mix_sums.turn(3)
    mix_sums.far(4)
    lax.fori_loop(2, 4, back, 0)

    d_kv = jnp.concatenate(
        [
            v.d_key_t[:HEAD_DIM] + v.d_key_t[HEAD_DIM:],
            v.d_value_t[0] + v.d_value_t[1],
        ],
        0,
    ).T
    first = low(d_kv.shape)
    d_key = jnp.where(first, d_kv, swap(d_kv)).astype(bf16).astype(f32)
    d_gained = rotate_back(d_key, v.cosine[...], v.sine[...])
    hat, scale = pair_normed(v.k_raw[...])
    v.gain[9:10, :] = jnp.sum(d_gained * hat, 0, keepdims=True)
    d_raw = pair_norm_back(d_gained * k_gain, hat, scale)
    v.d_qkv[:, 128:256] = jnp.where(first, d_raw, d_kv).astype(bf16)

    def spread(dy):
        def one(i, _):
            t = net.tp_at(dy, 1 - i)
            v.spare[rows_of(8 + t), :] = dot_nt(v.d_qkv[rows_of(t), :], v.w_qkv[...]).astype(bf16)
            return 0

        lax.fori_loop(0, 2, one, 0)

    grad_qkv = dot(v.h_t[...], v.d_qkv[...])
    for e in range(blocks):
        v.grad_terms[e, :, 0:256] = grad_qkv[e * block : (e + 1) * block].astype(bf16)
    grad_sums = ScatterEp(
        net,
        banks["ep0"],
        lambda e, start, count: v.grad_terms.at[e, pl.ds(start, count)],
        lambda i, start, count: v.grad_landed.at[i, pl.ds(start, count)],
        block,
    )
    for g in (3, 1, 2, 0):
        grad_sums.far(g)
    sums = token_sums()
    spread(2)
    sums.across(2)
    spread(1)
    sums.across(1)
    sums.far()
    spread(-1)
    sums.across(-1)
    for g in (3, 1, 2, 0):
        grad_sums.near(g)
    sums.near_first()
    spread(0)
    sums.across(0)
    products = grad_qkv * v.w_qkv[...].astype(f32)
    norm_sum = lax.dot_general(
        jnp.ones((8, 256), f32), products, (((1,), (1,)), ((), ())), precision=highest, preferred_element_type=f32
    )[0:1]
    norm_sum = norm_sum / v.norm_gain[...]
    for i in range(8):
        v.gain[i : i + 1, :] = norm_sum[:, i * 128 : (i + 1) * 128]
    gain_c = AxisSum(net, banks["gains"], v.gain.at[0:8], v.gain_got.at[0, :, 0:8], [C])
    sums.near_second()
    grad_sums.turn(3)
    grad_sums.far(4)
    small[mine, :] = small_y.finish()
    small_x = AxisSum(net, banks["small"], small.at[mine], v.small_got.at[1], ALONG_X)
    v.gain[0:8, :] = gain_c.finish()
    gain_y = AxisSum(net, banks["gains"], v.gain.at[0:8], v.gain_got.at[1, :, 0:8], ALONG_Y)
    grad_sums.turn(1)
    grad_sums.turn(2)
    grad_sums.near(4)
    grad_sums.turn(0)
    mix_sums.turn(1)
    mix_sums.turn(2)
    mix_sums.near(4)
    mix_sums.turn(0)
    for h in (0, 1):
        part = grad_sums.last(4, h).astype(bf16)
        v.grad_all[net.ep, h * (block // 2) : (h + 1) * (block // 2), :] = part
    spread_grads = GatherEp(net, banks["ep2"], v.grad_all, block)
    spread_grads.start()
    v.gain[0:8, :] = gain_y.finish()
    gain_x = AxisSum(net, banks["gains"], v.gain, v.gain_got.at[2], ALONG_X)
    small[mine, :] = small_x.finish()
    small_z = AxisSum(net, banks["small"], small.at[mine], v.small_got.at[2], ALONG_Z)

    x_hat, x_scale = normed(v.x[...].reshape(rows, width))
    total = jnp.concatenate([sums.last(0), sums.last(1)], 0)
    v.grad_input[...] = d_mid[...] + norm_back(total * v.norm_gain[...], x_hat, x_scale)

    spread_grads.first()
    spread_grads.second(0)
    spread_grads.far()
    v.gain[...] = gain_x.finish()
    gain_z = AxisSum(net, banks["gains"], v.gain, v.gain_got.at[3], ALONG_Z)
    spread_grads.second(-1)
    spread_grads.second(1)
    spread_grads.second(2)
    small[mine, :] = small_z.finish()
    small_last = net.send(small.at[mine], v.small_sib.at[mine], C, banks["small"])
    mix = jnp.concatenate([mix_sums.last(4, 0), mix_sums.last(4, 1)], 0)
    v.output[...] = jnp.where(place < seq_len, h_mid[...] + mix, 0.0)
    for out, sum_ in ((v.grad_gate, gate), (v.grad_up, up), (v.grad_down, down)):
        for j in (0, 1):
            out[j] = sum_.last(j)
    v.gain_out[...] = gain_z.finish()
    small_last.wait_recv()
    other = pl.ds(pl.multiple_of((1 - net.c) * share, 8), share)
    v.small_out[mine, :] = small[mine, :]
    v.small_out[other, :] = v.small_sib[other, :]
    prob_total = v.small_out[n_exp + 8 :, 0:n_exp]
    loss = jnp.dot(prob_total, counts, precision=highest, preferred_element_type=f32)
    v.loss[...] = loss * (n_exp / (8.0 * nvalid * nvalid)) + jnp.zeros((8, 128), f32)
    spread_grads.finish()
    for e in range(blocks):
        at = slice(e * block, (e + 1) * block)
        v.grad_query[at, :] = v.grad_all[e, :, 0:128].astype(f32)
        v.grad_keyval[at, :] = v.grad_all[e, :, 128:256].astype(f32)
    v.grad_out[...] = v.grad_all[:, :, 256:384].astype(f32).reshape(blocks * block, 128).T
    net.finish()


LARGE = ("output", "grad_input", "grad_query", "grad_keyval", "grad_out", "grad_gate", "grad_up", "grad_down")


def results_kernel(*refs):
    n = len(LARGE)
    large, (loss_in, gains, small), refs = refs[:n], refs[n : n + 3], refs[n + 3 :]
    out, (loss, norm_gain, query_gain, key_gain, mlp_gain, router), refs = refs[:n], refs[n : n + 6], refs[n + 6 :]
    held, sems = refs[:n], refs[n]
    reads = [pltpu.make_async_copy(large[i], held[i], sems.at[0, i]) for i in range(n)]
    for copy in reads:
        copy.start()
    n_exp = router.shape[0]
    loss[...] = loss_in[0:1, 0:1]
    for i in range(8):
        norm_gain[:, i * 128 : (i + 1) * 128] = gains[i : i + 1, :]
    query_gain[...] = gains[8:9, :]
    key_gain[...] = gains[9:10, 0:HEAD_DIM]
    mlp_gain[...] = small[n_exp : n_exp + 1, :]
    router[...] = small[0:n_exp, :]
    writes = []
    for i in range(n):
        reads[i].wait()
        writes.append(pltpu.make_async_copy(held[i], out[i], sems.at[1, i]))
        writes[i].start()
    for copy in writes:
        copy.wait()


def local(
    layer_input,
    lengths,
    routes,
    norm_gain,
    w_query,
    w_keyval,
    query_gain,
    key_gain,
    w_out,
    mlp_gain,
    w_router,
    w_gate,
    w_up,
    w_down,
    cotangent,
):
    rows, width = layer_input.shape
    group = rows * 8
    n_exp = w_router.shape[1]
    top_k = routes.shape[1]
    units = w_down.shape[1]
    ff = units * 8
    slots = 3 * rows * top_k // (2 * n_exp)
    full = 16 * slots
    n = BATCH * slots
    block = width // 16
    n_small = n_exp + 16
    cosine, sine = rotary(group)
    inputs = {
        "layer_input": (layer_input, ANY),
        "lengths": (lengths, SM),
        "routes_in": (routes.T, ANY),
        "norm_gain": (norm_gain.reshape(1, -1), VM),
        "w_query": (w_query, ANY),
        "w_keyval": (w_keyval.reshape(width, -1), ANY),
        "query_gain": (query_gain.reshape(1, -1), VM),
        "key_gain": (key_gain.reshape(1, -1), VM),
        "w_out_in": (w_out, ANY),
        "mlp_gain": (mlp_gain.reshape(1, -1), VM),
        "w_router_t": (w_router.T, VM),
        "w_gate": (w_gate.transpose(0, 2, 1), ANY),
        "w_up": (w_up.transpose(0, 2, 1), ANY),
        "w_down": (w_down, ANY),
        "cotangent": (cotangent, ANY),
        "cosine_in": (jnp.asarray(cosine), ANY),
        "sine_in": (jnp.asarray(sine), ANY),
    }
    outputs = {
        "output": (rows, width),
        "grad_input": (rows, width),
        "loss": (8, 128),
        "grad_query": (width, 128),
        "grad_keyval": (width, 128),
        "gain_out": (16, 128),
        "grad_out": (128, width),
        "small_out": (n_small, width),
        "grad_gate": (2, units, width),
        "grad_up": (2, units, width),
        "grad_down": (2, units, width),
    }
    eight = pltpu.VMEM((8, rows, width), bf16)
    sixteen = pltpu.VMEM((16, rows, width), bf16)
    row_bf = pltpu.VMEM((group, 128), bf16)
    row_f = pltpu.VMEM((group, 128), f32)
    piece = pltpu.VMEM((4, 4, 8, rows), f32)
    by_expert = pltpu.VMEM((n_exp, rows), f32)
    scratch = {
        "w_qkv": pltpu.VMEM((width, 256), bf16),
        "w_out": pltpu.VMEM((128, width), bf16),
        "cosine": row_f,
        "sine": row_f,
        "routes": pltpu.VMEM((top_k, 16 * group), jnp.int32),
        "w": pltpu.VMEM((2, 3 * ff, width), bf16),
        "k_gain": pltpu.VMEM((1, 128), f32),
        "h_t": pltpu.VMEM((width, group), bf16),
        "spare": pltpu.VMEM((16 * rows, width), bf16),
        "d_all": eight,
        "query": row_bf,
        "key": row_bf,
        "value": pltpu.VMEM((group, 256), bf16),
        "k_raw": row_f,
        "attn_o": row_bf,
        "from_sib": pltpu.VMEM((4, rows, width), bf16),
        "from_far": pltpu.VMEM((2, rows // 2, width), bf16),
        "from_near": pltpu.VMEM((2, rows, width), bf16),
        "tok": sixteen,
        "cot": sixteen,
        "hits": by_expert,
        "probs": by_expert,
        "soft": by_expert,
        "d_gates": by_expert,
        "places": pltpu.VMEM((16, 2 * slots, rows), bf16),
        "counted": pltpu.VMEM((n_exp, 8, 128), f32),
        "gate_out": piece,
        "gate_mid": piece,
        "gate_got": piece,
        "back_out": piece,
        "back_mid": piece,
        "back_got": piece,
        "big": pltpu.VMEM((4 * full, width), bf16),
        "deep": pltpu.VMEM((max(3 * full, 2 * group), 2 * ff), bf16),
        "row_back": pltpu.VMEM((2, n, width), bf16),
        "landed": pltpu.VMEM((30, rows // 2, width), bf16),
        "w_sib": pltpu.VMEM((4, 3, 2, units, width), bf16),
        "w_far": pltpu.VMEM((3, 2, units, width), bf16),
        "w_near": pltpu.VMEM((2, 3, 2, units, width), bf16),
        "small": pltpu.VMEM((n_small, width), f32),
        "small_sib": pltpu.VMEM((n_small, width), f32),
        "small_got": pltpu.VMEM((3, 3, n_small // 2, width), f32),
        "d_qkv": pltpu.VMEM((group, 256), bf16),
        "grad_terms": pltpu.VMEM((16, block, 384), bf16),
        "grad_landed": pltpu.VMEM((30, block // 2, 384), bf16),
        "grad_all": pltpu.VMEM((16, block, 384), bf16),
        "gain": pltpu.VMEM((16, 128), f32),
        "gain_got": pltpu.VMEM((4, 3, 16, 128), f32),
        "send_sems": pltpu.SemaphoreType.DMA((SENDS,)),
        "recv_sems": pltpu.SemaphoreType.DMA((sum(BANKS.values()),)),
    }
    got = pl.pallas_call(
        lambda *refs: layer_kernel(*refs, inputs=tuple(inputs), outputs=tuple(outputs), scratch=tuple(scratch)),
        name="layer",
        out_shape=tuple(shaped(shape, f32) for shape in outputs.values()),
        in_specs=[spec for _, spec in inputs.values()],
        out_specs=(VM,) * len(outputs),
        scratch_shapes=list(scratch.values()),
        compiler_params=params(1, 63.9),
    )(*[array for array, _ in inputs.values()])
    got = dict(zip(outputs, got, strict=True))
    large = [got[name] for name in LARGE]
    pieces = [got[name] for name in ("loss", "gain_out", "small_out")]
    sizes = [(1, 1), (1, width), (1, 128), (1, HEAD_DIM), (1, width), (n_exp, width)]
    got = pl.pallas_call(
        results_kernel,
        name="results",
        out_shape=tuple(shaped(a.shape, f32) for a in large) + tuple(shaped(size, f32) for size in sizes),
        in_specs=[pl.BlockSpec(memory_space=pltpu.HBM)] * len(large) + [VM] * len(pieces),
        out_specs=(ANY,) * len(large) + (VM,) * len(sizes),
        scratch_shapes=[pltpu.VMEM(a.shape, f32) for a in large] + [pltpu.SemaphoreType.DMA((2, len(large)))],
        compiler_params=pltpu.CompilerParams(vmem_limit_bytes=62 * MIB),
    )(*large, *pieces)
    large = dict(zip(LARGE, got, strict=False))
    loss, grad_norm_gain, grad_query_gain, grad_key_gain, grad_mlp_gain, grad_router = got[len(LARGE) :]
    return (
        large["output"],
        large["grad_input"],
        loss.reshape(()),
        grad_norm_gain.reshape(-1),
        large["grad_query"],
        large["grad_keyval"].reshape(w_keyval.shape),
        grad_query_gain.reshape(-1),
        grad_key_gain.reshape(-1),
        large["grad_out"],
        grad_mlp_gain.reshape(-1),
        grad_router.T,
        large["grad_gate"].transpose(0, 2, 1),
        large["grad_up"].transpose(0, 2, 1),
        large["grad_down"],
    )


def solution(mesh):
    in_specs = (
        P(("ep", "tp"), None),
        P(),
        P(),
        P(),
        P(None, "tp"),
        P(None, "tp", None),
        P("tp"),
        P("tp"),
        P("tp", None),
        P(),
        P(),
        P("ep", None, "tp"),
        P("ep", None, "tp"),
        P("ep", "tp", None),
        P(("ep", "tp"), None),
    )
    out_specs = (
        P(("ep", "tp"), None),
        P(("ep", "tp"), None),
        P(),
        P(),
        P(None, "tp"),
        P(None, "tp", None),
        P("tp"),
        P("tp"),
        P("tp", None),
        P(),
        P(),
        P("ep", None, "tp"),
        P("ep", None, "tp"),
        P("ep", "tp", None),
    )
    return jax.shard_map(local, mesh=mesh, in_specs=in_specs, out_specs=out_specs, check_vma=False)
```

profile of v0, /device:TPU:0, one launch (start us, length us, event | category | flops | bytes accessed | tf_op | source)
XLA Modules:
  0.0 177.3 jit_solution(2058747460192050349)
XLA Ops:
  0.7 171.3 %layer.1 = (f32[128,1024]{1,0:T(8,128)}, f32[128,1024]{1,0:T(8,128)}, f32[8,128]{1,0:T(8,128)}, f32[1024,128]{1,0:T(8,128)}, f32[1024,128]{1,0:T(8,128)}, /*inde...) custom-call(f32[128,1024]{1,0:T(8,128)} %refs_0_.1, ...), custom_call_target="tpu_custom_call" | custom-call | tf_op jit(solution)/shard_map/layer/pallas_call | solution.py:1239
  171.9 5.2 %results.1 = (f32[128,1024]{1,0:T(8,128)}, f32[128,1024]{1,0:T(8,128)}, f32[1024,128]{1,0:T(8,128)}, f32[1024,128]{1,0:T(8,128)}, f32[128,1024]{1,0:T(8,128)}, /...) custom-call(f32[128,1024]{1,0:T(8,128)} %get-tuple-element.39.refs_0, ...), custom_call_target="tpu_custom_call" | custom-call | tf_op jit(solution)/shard_map/results/pallas_call | solution.py:1252
where the time goes:
time: 177 us
  Pallas kernels  176 us (99%)
    pallas_call x1, Pallas kernels, local(): pl.pallas_call(lambda *refs: layer_kernel(*refs, inputs=tuple(inputs), ou...  171 us
    pallas_call x1, Pallas kernels, local(): pl.pallas_call(results_kernel, name='results', out_shape=tuple((shaped(a....  5.21 us

commit v1 on v0

--- a/solution.py
+++ b/solution.py
@@ -473,10 +473,10 @@
         self.copies = [net.send(term, slots.at[i], d, bank) for i, d in enumerate(steps)]
 
     def finish(self):
-        total = self.term[...]
+        total = self.term[...].astype(f32)
         for i, copy in enumerate(self.copies):
             copy.wait_recv()
-            total = total + self.slots[i]
+            total = total + self.slots[i].astype(f32)
             self.net.sent(copy)
         return total
 
@@ -634,7 +634,6 @@
         GatherTp(net, banks[f"gather{a}"], lambda t, half, a=a: weight(a, half, t)) for a in range(3)
     )
     w_step(gate.start)
-    w_step(up.start)
     tokens.need(2, 1)
     project(2)
     tokens.finish()
@@ -683,8 +682,9 @@
     sums.near_first()
     attend(0)
     sums.across(0)
+    sums.near_second()
     w_step(gate.relay)
-    sums.near_second()
+    w_step(up.start)
     cots_step(cots.second, 1)
     cots_step(cots.second, 2)
     h_mid = v.output
@@ -836,9 +836,6 @@
         return 0
 
     lax.fori_loop(0, 2, grads, 0)
-    to_tokens.turn()
-    for g in (3, 1, 2):
-        row_sums.near(g)
     gate, up, down = (
         ScatterTp(
             net,
@@ -853,14 +850,19 @@
     for dy in (2, 1, -1, 0):
         for sum_ in (gate, up, down):
             w_step(sum_.across, dy)
+    to_tokens.turn()
+    for g in (3, 1, 2):
+        row_sums.near(g)
+    for sum_ in (gate, up, down):
+        w_step(sum_.far)
+    for sum_ in (gate, up, down):
+        w_step(sum_.near_first)
     for s in range(16):
         i = net.ep_at(*ORDER[s])
         both = jnp.concatenate([v.spare[picked(j, s * slots, slots), :] for j in (0, 1)], 0)
         v.big[rows_of(i), :] = dot_tn(v.places[i], both).astype(bf16)
     row_sums.turn(3)
     row_sums.far(4)
-    for sum_ in (gate, up, down):
-        w_step(sum_.far)
     to_tokens.finish()
 
     for e in range(16):
@@ -880,12 +882,13 @@
     )
     h_hat, h_scale = normed(h_mid[...])
     mlp_in = h_hat * v.mlp_gain[...]
-    small = v.small
-    small[0:n_exp, :] = jnp.dot(d_logits, mlp_in, precision=highest, preferred_element_type=f32)
-    small[n_exp + 8 :, :] = jnp.zeros((8, width), f32)
-    small[n_exp + 8 :, 0:n_exp] = lax.dot_general(
+    small, gain = v.small, v.gain
+    small[...] = jnp.dot(d_logits, mlp_in, precision=highest, preferred_element_type=f32).astype(bf16)
+    gain[...] = jnp.zeros_like(gain)
+    gain[16:24, 0:n_exp] = lax.dot_general(
         valid + jnp.zeros((8, rows), f32), probs, (((1,), (1,)), ((), ())), precision=highest, preferred_element_type=f32
     )
+    small_first = net.send(small, v.small_sib, C, banks["small"])
     row_sums.turn(1)
     row_sums.turn(2)
     row_sums.near(4)
@@ -894,7 +897,8 @@
     total = jnp.concatenate([row_sums.last(4, 0), row_sums.last(4, 1)], 0)
     d_mlp_in = d_mlp_in + total
     gain_grad = jnp.sum(d_mlp_in * h_hat, 0, keepdims=True)
-    small[n_exp : n_exp + 8, :] = gain_grad + jnp.zeros((8, width), f32)
+    for i in range(8):
+        gain[8 + i : 9 + i, :] = gain_grad[:, i * 128 : (i + 1) * 128]
     d_mid = v.grad_input
     d_mid[...] = d_out + norm_back(d_mlp_in * v.mlp_gain[...], h_hat, h_scale)
 
@@ -908,7 +912,6 @@
         mix_sums.far(g)
     net.group = None
     share = small.shape[0] // 2
-    small_first = net.send(small, v.small_sib, C, banks["small"])
     v.d_key_t[...] = jnp.zeros_like(v.d_key_t)
     v.d_value_t[...] = jnp.zeros_like(v.d_value_t)
 
@@ -918,22 +921,24 @@
             v.deep[rows_of(head * 8 + i), :] = weights_of(q, head)
         return 0
 
-    lax.fori_loop(0, 8, softmax_of, 0)
-    tokens.relay()
+    lax.fori_loop(0, 4, softmax_of, 0)
     small_first.wait_recv()
     net.sent(small_first)
-    mine = pl.ds(pl.multiple_of(net.c * share, 8), share)
+    mine = pl.ds(pl.multiple_of(net.c * share, share), share)
     small[mine, :] = small[mine, :] + v.small_sib[mine, :]
+    tokens.relay()
+    small_y = AxisSum(net, banks["small"], small.at[mine], v.small_got.at[0], ALONG_Y)
+    lax.fori_loop(4, 8, softmax_of, 0)
+    tokens.share()
     net.group = "mix"
     for g in (3, 1, 2, 0):
         mix_sums.near(g)
     net.group = None
-    tokens.share()
     tokens.spread()
+    small[mine, :] = small_y.finish().astype(bf16)
+    small_x = AxisSum(net, banks["small"], small.at[mine], v.small_got.at[1], ALONG_X)
     for sum_ in (gate, up, down):
-        w_step(sum_.near_first)
         w_step(sum_.near_second)
-    small_y = AxisSum(net, banks["small"], small.at[mine], v.small_got.at[0], ALONG_Y)
     tokens.finish()
 
     def back(i, _):
@@ -958,11 +963,10 @@
         d_query = (jnp.where(first, d_q[0], d_q[1]) * factor).astype(bf16).astype(f32)
         d_gained = rotate_back(d_query, v.cosine[at, :], v.sine[at, :])
         hat, scale = pair_normed(v.q_raw[at, :])
-        v.gain[8:9, :] += jnp.sum(d_gained * hat, 0, keepdims=True)
+        v.gain[24:25, :] += jnp.sum(d_gained * hat, 0, keepdims=True)
         v.d_qkv[at, 0:128] = pair_norm_back(d_gained * q_gain, hat, scale).astype(bf16)
         return 0
 
-    v.gain[...] = jnp.zeros_like(v.gain)
     lax.fori_loop(0, 2, back, 0)
     blocks, block = v.grad_terms.shape[0], v.grad_terms.shape[1]
     grad_o = dot_tn(v.attn_o[...], v.d_all[...].reshape(group, width)).T
@@ -970,6 +974,8 @@
         v.grad_terms[e, :, 256:384] = grad_o[e * block : (e + 1) * block].astype(bf16)
     mix_sums.turn(3)
     mix_sums.far(4)
+    small[mine, :] = small_x.finish().astype(bf16)
+    small_z = AxisSum(net, banks["small"], small.at[mine], v.small_got.at[2], ALONG_Z)
     lax.fori_loop(2, 4, back, 0)
 
     d_kv = jnp.concatenate(
@@ -983,7 +989,7 @@
     d_key = jnp.where(first, d_kv, swap(d_kv)).astype(bf16).astype(f32)
     d_gained = rotate_back(d_key, v.cosine[...], v.sine[...])
     hat, scale = pair_normed(v.k_raw[...])
-    v.gain[9:10, :] = jnp.sum(d_gained * hat, 0, keepdims=True)
+    v.gain[25:26, :] = jnp.sum(d_gained * hat, 0, keepdims=True)
     d_raw = pair_norm_back(d_gained * k_gain, hat, scale)
     v.d_qkv[:, 128:256] = jnp.where(first, d_raw, d_kv).astype(bf16)
 
@@ -1020,42 +1026,36 @@
     sums.near_first()
     spread(0)
     sums.across(0)
-    products = grad_qkv * v.w_qkv[...].astype(f32)
-    norm_sum = lax.dot_general(
-        jnp.ones((8, 256), f32), products, (((1,), (1,)), ((), ())), precision=highest, preferred_element_type=f32
-    )[0:1]
-    norm_sum = norm_sum / v.norm_gain[...]
-    for i in range(8):
-        v.gain[i : i + 1, :] = norm_sum[:, i * 128 : (i + 1) * 128]
-    gain_c = AxisSum(net, banks["gains"], v.gain.at[0:8], v.gain_got.at[0, :, 0:8], [C])
-    sums.near_second()
-    grad_sums.turn(3)
-    grad_sums.far(4)
-    small[mine, :] = small_y.finish()
-    small_x = AxisSum(net, banks["small"], small.at[mine], v.small_got.at[1], ALONG_X)
-    v.gain[0:8, :] = gain_c.finish()
-    gain_y = AxisSum(net, banks["gains"], v.gain.at[0:8], v.gain_got.at[1, :, 0:8], ALONG_Y)
-    grad_sums.turn(1)
-    grad_sums.turn(2)
-    grad_sums.near(4)
-    grad_sums.turn(0)
     mix_sums.turn(1)
     mix_sums.turn(2)
     mix_sums.near(4)
     mix_sums.turn(0)
+    sums.near_second()
+    grad_sums.turn(3)
+    grad_sums.far(4)
+    products = (grad_qkv * v.w_qkv[...].astype(f32)).astype(bf16)
+    norm_sum = dot_nt(jnp.ones((16, 256), bf16), products)[0:1] / v.norm_gain[...]
+    for i in range(8):
+        v.gain[i : i + 1, :] = norm_sum[:, i * 128 : (i + 1) * 128]
+    gain_c = AxisSum(net, banks["gains"], v.gain.at[0:24], v.gain_got.at[0, :, 0:24], [C])
+    grad_sums.turn(1)
+    v.gain[0:24, :] = gain_c.finish()
+    gain_y = AxisSum(net, banks["gains"], v.gain.at[0:24], v.gain_got.at[1, :, 0:24], ALONG_Y)
+    grad_sums.turn(2)
+    grad_sums.near(4)
+    grad_sums.turn(0)
     for h in (0, 1):
         part = grad_sums.last(4, h).astype(bf16)
         v.grad_all[net.ep, h * (block // 2) : (h + 1) * (block // 2), :] = part
     spread_grads = GatherEp(net, banks["ep2"], v.grad_all, block)
     spread_grads.start()
-    v.gain[0:8, :] = gain_y.finish()
+    v.gain[0:24, :] = gain_y.finish()
     gain_x = AxisSum(net, banks["gains"], v.gain, v.gain_got.at[2], ALONG_X)
-    small[mine, :] = small_x.finish()
-    small_z = AxisSum(net, banks["small"], small.at[mine], v.small_got.at[2], ALONG_Z)
 
     x_hat, x_scale = normed(v.x[...].reshape(rows, width))
     total = jnp.concatenate([sums.last(0), sums.last(1)], 0)
     v.grad_input[...] = d_mid[...] + norm_back(total * v.norm_gain[...], x_hat, x_scale)
+    leaving = [net.keep(v.grad_input, v.grad_input_out)]
 
     spread_grads.first()
     spread_grads.second(0)
@@ -1065,54 +1065,67 @@
     spread_grads.second(-1)
     spread_grads.second(1)
     spread_grads.second(2)
-    small[mine, :] = small_z.finish()
+    small[mine, :] = small_z.finish().astype(bf16)
     small_last = net.send(small.at[mine], v.small_sib.at[mine], C, banks["small"])
     mix = jnp.concatenate([mix_sums.last(4, 0), mix_sums.last(4, 1)], 0)
     v.output[...] = jnp.where(place < seq_len, h_mid[...] + mix, 0.0)
-    for out, sum_ in ((v.grad_gate, gate), (v.grad_up, up), (v.grad_down, down)):
+    leaving.append(net.keep(v.output, v.output_out))
+    for out, to, sum_ in (
+        (v.grad_gate, v.grad_gate_out, gate),
+        (v.grad_up, v.grad_up_out, up),
+        (v.grad_down, v.grad_down_out, down),
+    ):
         for j in (0, 1):
             out[j] = sum_.last(j)
+        leaving.append(net.keep(out, to))
     v.gain_out[...] = gain_z.finish()
     small_last.wait_recv()
-    other = pl.ds(pl.multiple_of((1 - net.c) * share, 8), share)
-    v.small_out[mine, :] = small[mine, :]
-    v.small_out[other, :] = v.small_sib[other, :]
-    prob_total = v.small_out[n_exp + 8 :, 0:n_exp]
+    other = pl.ds(pl.multiple_of((1 - net.c) * share, share), share)
+    v.small_out[mine, :] = small[mine, :].astype(f32)
+    v.small_out[other, :] = v.small_sib[other, :].astype(f32)
+    prob_total = v.gain_out[16:24, 0:n_exp]
     loss = jnp.dot(prob_total, counts, precision=highest, preferred_element_type=f32)
     v.loss[...] = loss * (n_exp / (8.0 * nvalid * nvalid)) + jnp.zeros((8, 128), f32)
     spread_grads.finish()
-    for e in range(blocks):
-        at = slice(e * block, (e + 1) * block)
-        v.grad_query[at, :] = v.grad_all[e, :, 0:128].astype(f32)
-        v.grad_keyval[at, :] = v.grad_all[e, :, 128:256].astype(f32)
-    v.grad_out[...] = v.grad_all[:, :, 256:384].astype(f32).reshape(blocks * block, 128).T
+    leaving.append(net.keep(v.grad_all, v.grads_out))
+    for copy in leaving:
+        net.kept(copy)
     net.finish()
 
 
-LARGE = ("output", "grad_input", "grad_query", "grad_keyval", "grad_out", "grad_gate", "grad_up", "grad_down")
+LARGE = ("output", "grad_input", "grad_gate", "grad_up", "grad_down")
 
 
 def results_kernel(*refs):
     n = len(LARGE)
-    large, (loss_in, gains, small), refs = refs[:n], refs[n : n + 3], refs[n + 3 :]
-    out, (loss, norm_gain, query_gain, key_gain, mlp_gain, router), refs = refs[:n], refs[n : n + 6], refs[n + 6 :]
-    held, sems = refs[:n], refs[n]
+    large, (grads_in, loss_in, gains, small), refs = refs[:n], refs[n : n + 4], refs[n + 4 :]
+    out, made, refs = refs[:n], refs[n : n + 3], refs[n + 3 :]
+    (loss, norm_gain, query_gain, key_gain, mlp_gain, router), refs = refs[:6], refs[6:]
+    held, grads, parts, sems = refs[:n], refs[n], refs[n + 1 : n + 4], refs[n + 4]
+    grads_read = pltpu.make_async_copy(grads_in, grads, sems.at[0, n])
+    grads_read.start()
     reads = [pltpu.make_async_copy(large[i], held[i], sems.at[0, i]) for i in range(n)]
     for copy in reads:
         copy.start()
-    n_exp = router.shape[0]
     loss[...] = loss_in[0:1, 0:1]
     for i in range(8):
         norm_gain[:, i * 128 : (i + 1) * 128] = gains[i : i + 1, :]
-    query_gain[...] = gains[8:9, :]
-    key_gain[...] = gains[9:10, 0:HEAD_DIM]
-    mlp_gain[...] = small[n_exp : n_exp + 1, :]
-    router[...] = small[0:n_exp, :]
+        mlp_gain[:, i * 128 : (i + 1) * 128] = gains[8 + i : 9 + i, :]
+    query_gain[...] = gains[24:25, :]
+    key_gain[...] = gains[25:26, 0:HEAD_DIM]
+    router[...] = small[...]
     writes = []
     for i in range(n):
         reads[i].wait()
         writes.append(pltpu.make_async_copy(held[i], out[i], sems.at[1, i]))
         writes[i].start()
+    grads_read.wait()
+    blocks, block, _ = grads.shape
+    for i in range(3):
+        part = grads[:, :, i * 128 : (i + 1) * 128].astype(f32).reshape(blocks * block, 128)
+        parts[i][...] = part if i < 2 else part.T
+        writes.append(pltpu.make_async_copy(parts[i], made[i], sems.at[1, n + i]))
+        writes[n + i].start()
     for copy in writes:
         copy.wait()
 
@@ -1144,7 +1157,6 @@
     full = 16 * slots
     n = BATCH * slots
     block = width // 16
-    n_small = n_exp + 16
     cosine, sine = rotary(group)
     inputs = {
         "layer_input": (layer_input, ANY),
@@ -1166,17 +1178,15 @@
         "sine_in": (jnp.asarray(sine), ANY),
     }
     outputs = {
-        "output": (rows, width),
-        "grad_input": (rows, width),
-        "loss": (8, 128),
-        "grad_query": (width, 128),
-        "grad_keyval": (width, 128),
-        "gain_out": (16, 128),
-        "grad_out": (128, width),
-        "small_out": (n_small, width),
-        "grad_gate": (2, units, width),
-        "grad_up": (2, units, width),
-        "grad_down": (2, units, width),
+        "output_out": (shaped((rows, width), f32), ANY),
+        "grad_input_out": (shaped((rows, width), f32), ANY),
+        "grad_gate_out": (shaped((2, units, width), f32), ANY),
+        "grad_up_out": (shaped((2, units, width), f32), ANY),
+        "grad_down_out": (shaped((2, units, width), f32), ANY),
+        "grads_out": (shaped((16, block, 384), bf16), ANY),
+        "loss": (shaped((8, 128), f32), VM),
+        "gain_out": (shaped((32, 128), f32), VM),
+        "small_out": (shaped((n_exp, width), f32), VM),
     }
     eight = pltpu.VMEM((8, rows, width), bf16)
     sixteen = pltpu.VMEM((16, rows, width), bf16)
@@ -1192,6 +1202,14 @@
         "routes": pltpu.VMEM((top_k, 16 * group), jnp.int32),
         "w": pltpu.VMEM((2, 3 * ff, width), bf16),
         "k_gain": pltpu.VMEM((1, 128), f32),
+        "output": pltpu.VMEM((rows, width), f32),
+        "grad_input": pltpu.VMEM((rows, width), f32),
+        "grad_query": row_f,
+        "grad_keyval": row_f,
+        "grad_out": pltpu.VMEM((128, width), f32),
+        "grad_gate": pltpu.VMEM((2, units, width), f32),
+        "grad_up": pltpu.VMEM((2, units, width), f32),
+        "grad_down": pltpu.VMEM((2, units, width), f32),
         "h_t": pltpu.VMEM((width, group), bf16),
         "spare": pltpu.VMEM((16 * rows, width), bf16),
         "d_all": eight,
@@ -1224,42 +1242,45 @@
         "w_sib": pltpu.VMEM((4, 3, 2, units, width), bf16),
         "w_far": pltpu.VMEM((3, 2, units, width), bf16),
         "w_near": pltpu.VMEM((2, 3, 2, units, width), bf16),
-        "small": pltpu.VMEM((n_small, width), f32),
-        "small_sib": pltpu.VMEM((n_small, width), f32),
-        "small_got": pltpu.VMEM((3, 3, n_small // 2, width), f32),
+        "small": pltpu.VMEM((n_exp, width), bf16),
+        "small_sib": pltpu.VMEM((n_exp, width), bf16),
+        "small_got": pltpu.VMEM((3, 3, n_exp // 2, width), bf16),
         "d_qkv": pltpu.VMEM((group, 256), bf16),
         "grad_terms": pltpu.VMEM((16, block, 384), bf16),
         "grad_landed": pltpu.VMEM((30, block // 2, 384), bf16),
         "grad_all": pltpu.VMEM((16, block, 384), bf16),
-        "gain": pltpu.VMEM((16, 128), f32),
-        "gain_got": pltpu.VMEM((4, 3, 16, 128), f32),
+        "gain": pltpu.VMEM((32, 128), f32),
+        "gain_got": pltpu.VMEM((4, 3, 32, 128), f32),
         "send_sems": pltpu.SemaphoreType.DMA((SENDS,)),
         "recv_sems": pltpu.SemaphoreType.DMA((sum(BANKS.values()),)),
     }
     got = pl.pallas_call(
         lambda *refs: layer_kernel(*refs, inputs=tuple(inputs), outputs=tuple(outputs), scratch=tuple(scratch)),
         name="layer",
-        out_shape=tuple(shaped(shape, f32) for shape in outputs.values()),
+        out_shape=tuple(shape for shape, _ in outputs.values()),
         in_specs=[spec for _, spec in inputs.values()],
-        out_specs=(VM,) * len(outputs),
+        out_specs=tuple(spec for _, spec in outputs.values()),
         scratch_shapes=list(scratch.values()),
         compiler_params=params(1, 63.9),
     )(*[array for array, _ in inputs.values()])
     got = dict(zip(outputs, got, strict=True))
-    large = [got[name] for name in LARGE]
+    large = [got[name + "_out"] for name in LARGE] + [got["grads_out"]]
     pieces = [got[name] for name in ("loss", "gain_out", "small_out")]
+    made = [(width, 128), (width, 128), (128, width)]
     sizes = [(1, 1), (1, width), (1, 128), (1, HEAD_DIM), (1, width), (n_exp, width)]
     got = pl.pallas_call(
         results_kernel,
         name="results",
-        out_shape=tuple(shaped(a.shape, f32) for a in large) + tuple(shaped(size, f32) for size in sizes),
+        out_shape=tuple(shaped(a.shape, f32) for a in large[:-1]) + tuple(shaped(size, f32) for size in made + sizes),
         in_specs=[pl.BlockSpec(memory_space=pltpu.HBM)] * len(large) + [VM] * len(pieces),
-        out_specs=(ANY,) * len(large) + (VM,) * len(sizes),
-        scratch_shapes=[pltpu.VMEM(a.shape, f32) for a in large] + [pltpu.SemaphoreType.DMA((2, len(large)))],
+        out_specs=(ANY,) * (len(LARGE) + len(made)) + (VM,) * len(sizes),
+        scratch_shapes=[pltpu.VMEM(a.shape, a.dtype) for a in large]
+        + [pltpu.VMEM(size, f32) for size in made]
+        + [pltpu.SemaphoreType.DMA((2, len(large) + len(made)))],
         compiler_params=pltpu.CompilerParams(vmem_limit_bytes=62 * MIB),
     )(*large, *pieces)
-    large = dict(zip(LARGE, got, strict=False))
-    loss, grad_norm_gain, grad_query_gain, grad_key_gain, grad_mlp_gain, grad_router = got[len(LARGE) :]
+    large = dict(zip(LARGE + ("grad_query", "grad_keyval", "grad_out"), got, strict=False))
+    loss, grad_norm_gain, grad_query_gain, grad_key_gain, grad_mlp_gain, grad_router = got[len(large) :]
     return (
         large["output"],
         large["grad_input"],

time: 177 us -> 169 us (0.955)
  Pallas kernels: 176 us -> 168 us
    pallas_call x1, Pallas kernels: 171 us -> 163 us  [local(): pl.pallas_call(lambda *refs: layer_kernel(*refs, inputs=tuple(inputs), ou...]
where the time goes in v1:
time: 169 us
  Pallas kernels  168 us (99%)
    pallas_call x1, Pallas kernels, local(): pl.pallas_call(lambda *refs: layer_kernel(*refs, inputs=tuple(inputs), ou...  163 us
    pallas_call x1, Pallas kernels, local(): pl.pallas_call(results_kernel, name='results', out_shape=tuple((shaped(a....  5.05 us

profile of v1, /device:TPU:0, one launch (start us, length us, event | category | flops | bytes accessed | tf_op | source)
XLA Modules:
  0.0 168.8 jit_solution(12580517461899147470)
XLA Ops:
  0.7 162.9 %layer.1 = (f32[128,1024]{1,0:T(8,128)}, f32[128,1024]{1,0:T(8,128)}, f32[2,64,1024]{2,1,0:T(8,128)}, f32[2,64,1024]{2,1,0:T(8,128)}, f32[2,64,1024]{2,1,0:T(8,1...) custom-call(f32[128,1024]{1,0:T(8,128)} %refs_0_.1, ...), custom_call_target="tpu_custom_call" | custom-call | tf_op jit(solution)/shard_map/layer/pallas_call | solution.py:1257
  163.6 5.0 %results.1 = (f32[128,1024]{1,0:T(8,128)}, f32[128,1024]{1,0:T(8,128)}, f32[2,64,1024]{2,1,0:T(8,128)}, f32[2,64,1024]{2,1,0:T(8,128)}, f32[2,64,1024]{2,1,0:T(8...) custom-call(f32[128,1024]{1,0:T(8,128)} %get-tuple-element.37.refs_0, ...), custom_call_target="tpu_custom_call" | custom-call | tf_op jit(solution)/shard_map/results/pallas_call | solution.py:1271
